TPU v7x, 32 devices: a whole 2x2x4 slice. The times are simulated.
32 devices in a mesh: group: 4 (over x, core), dp: 2 (over y), tensor: 4 (over z).
Axes of the slice: x: 2, y: 2, z: 4, core: 2. Of those that a mesh axis runs over, the one named last changes fastest.
Arguments:
- weight: float32 [14848, 8192], P('group', ('dp', 'tensor')), may hold values from -0.046875 to 0.046875
- moment: float32 [14848, 8192], P('group', ('dp', 'tensor')), may hold values from -1.8 to 1.8
- second: float32 [14848, 8192], P('group', ('dp', 'tensor')), may hold values from 0.02 to 0.3
- gradient: bfloat16 [14848, 8192], P('group', ('dp', 'tensor')), may hold values from -600 to 600
- hidden: bfloat16 [1024, 14848], P(('group', 'dp'), 'tensor'), may hold values from -6 to 6
- stream: bfloat16 [1024, 8192], P(('group', 'dp'), 'tensor'), may hold values from -32 to 32
- norm_gain: bfloat16 [8192], P('tensor'), may hold values from 0.25 to 1.75
Outputs:
- weight_new: float32 [14848, 8192], P('group', ('dp', 'tensor'))
- moment_new: float32 [14848, 8192], P('group', ('dp', 'tensor'))
- second_new: float32 [14848, 8192], P('group', ('dp', 'tensor'))
- normed: bfloat16 [1024, 8192], P(('group', 'dp'), 'tensor')
- residual: bfloat16 [1024, 8192], P(('group', 'dp'), 'tensor')
All inputs are finite; a program needn't handle non-finite values.
Results may differ from a plain program's by a relative error of at most 0.0095.
Values may be sent and summed in bfloat16 or wider, within the bound.
A program may use at most 256 MiB of HBM per device.

v0:
```python
import math

import jax
import jax.numpy as jnp
from jax import lax
from jax.sharding import PartitionSpec as P

D = 8192
FFW = 14848


clip_rms = 0.5
beta_one = 0.9
beta_two = 0.95
bias_one = 1.0 - 0.9**10
bias_two = 1.0 - 0.95**10
adam_eps = 1e-08
learn_rate = 0.002


def per_device(weight, moment, second, gradient, hidden, stream, norm_gain):
    grad_float = gradient.astype(jnp.float32)
    grad_total = lax.psum(jnp.sum(grad_float * grad_float), ("group", "dp", "tensor"))
    factor = jnp.minimum(1.0, clip_rms * math.sqrt(FFW * D) / (jnp.sqrt(grad_total) + 1e-06))
    clipped = factor * grad_float
    moment_new = beta_one * moment + (1.0 - beta_one) * clipped
    second_new = beta_two * second + (1.0 - beta_two) * clipped * clipped
    update = moment_new / bias_one / (jnp.sqrt(second_new / bias_two) + adam_eps)
    weight_new = weight - learn_rate * update
    shipped = weight_new.astype(jnp.bfloat16)
    owners = lax.axis_size("group")
    rank_count = lax.axis_size("dp")
    slices = lax.axis_size("tensor")
    rows_local, cols_local = shipped.shape
    per_owner = slices // owners
    owner_rows = rows_local // slices
    pieces = shipped.reshape(per_owner, owners, owner_rows, cols_local).transpose(1, 0, 2, 3)
    regrouped = lax.all_to_all(pieces, "group", split_axis=0, concat_axis=0, tiled=True)
    halves = owner_rows // rank_count
    arranged = regrouped.reshape(slices, rank_count, halves, cols_local)
    arranged = arranged.transpose(1, 0, 2, 3).reshape(rank_count * slices, halves, cols_local)
    received = lax.all_to_all(arranged, ("dp", "tensor"), split_axis=0, concat_axis=2, tiled=True)
    partial_value = jnp.dot(
        hidden,
        lax.all_gather(received[0], ("group", "dp"), axis=0, tiled=True),
        preferred_element_type=jnp.float32,
    )
    summed = lax.psum_scatter(
        partial_value.astype(jnp.bfloat16), "tensor", scatter_dimension=1, tiled=True
    ).astype(jnp.float32)
    residual_sum = stream.astype(jnp.float32) + summed
    squares = lax.psum(jnp.sum(residual_sum * residual_sum, axis=1), "tensor")
    normed = residual_sum * lax.rsqrt(squares / D + 1e-06)[:, None] * norm_gain.astype(jnp.float32)
    return (
        weight_new,
        moment_new,
        second_new,
        normed.astype(jnp.bfloat16),
        residual_sum.astype(jnp.bfloat16),
    )


def solution(mesh):
    placed = (
        P("group", ("dp", "tensor")),
        P("group", ("dp", "tensor")),
        P("group", ("dp", "tensor")),
        P("group", ("dp", "tensor")),
        P(("group", "dp"), "tensor"),
        P(("group", "dp"), "tensor"),
        P("tensor"),
    )
    return jax.shard_map(
        per_device,
        mesh=mesh,
        in_specs=placed,
        out_specs=(
            P("group", ("dp", "tensor")),
            P("group", ("dp", "tensor")),
            P("group", ("dp", "tensor")),
            P(("group", "dp"), "tensor"),
            P(("group", "dp"), "tensor"),
        ),
        check_vma=False,
    )
```

profile of v0, /device:TPU:0, one launch (start us, length us, event | category | flops | bytes accessed | tf_op | source)
XLA Modules:
  0.0 727.7 jit_solution(7217518674967683866)
XLA Ops:
  7.2 0.0 copy-start
  7.2 0.0 all-gather.2.cloned.1.call-start
  7.2 7.7 %fusion.2 = f32[]{:T(128)} fusion(bf16[3712,1024]{1,0:T(8,128)(2,1)} %param.10), kind=kLoop, calls=%fused_computation.5 | loop fusion | flops 11403263 | bytes 7602180 | tf_op jit(solution)/shard_map/reduce_sum | solution.py:23
  15.0 42.2 %psum.14 = f32[]{:T(128)} all-reduce(f32[]{:T(128)} %fusion.2), channel_id=1, replica_groups=mesh['group'=4,'dp'=2,'tensor'=4] {'group','dp','tensor'}, use_global_device_ids=true, to_apply=%region_1.0 | all-reduce | flops 1 | bytes 8 | tf_op jit(solution)/shard_map/psum | solution.py:23
  57.9 36.0 %fusion.6 = (bf16[3712,1024]{1,0:T(8,128)(2,1)}, f32[3712,1024]{1,0:T(8,128)}, f32[3712,1024]{1,0:T(8,128)}, f32[3712,1024]{1,0:T(8,128)}) fusion(f32[3712,1024]{1,0:T(8,128)} %param.7, bf16[3712,1024]{1,0:T(8,128)(2,1)} %param.10, f32[]{:T(128)S(6)} %min_shard_map.3, f32[3712,1024]{1,0:T(8,128)} %param.8, f32[3712,1024]{1,0:T(8,128)} %param.9), kind=kLoop, calls=%fused_computation.15 | loop fusion | flops 60817408 | bytes 106430464 | tf_op jit(solution)/shard_map/convert_element_type | solution.py:30
  93.9 88.7 %all_to_all.20 = bf16[4,1,928,1024]{3,2,1,0:T(8,128)(2,1)S(1)} all-to-all(bf16[4,1,928,1024]{3,2,1,0:T(8,128)(2,1)} %bitcast.21), channel_id=1, replica_groups=mesh['group'=4,'dp'=2,'tensor'=4] {'group'}, dimensions={0} | all-to-all | bytes 15204352 | tf_op jit(solution)/shard_map/all_to_all | solution.py:38
  182.7 4.0 copy.25
  186.7 172.6 %all_to_all.21 = bf16[8,464,1024]{2,1,0:T(8,128)(2,1)S(1)} all-to-all(bf16[8,464,1024]{2,1,0:T(8,128)(2,1)} %bitcast.19), channel_id=1, replica_groups=mesh['group'=4,'dp'=2,'tensor'=4] {'dp','tensor'}, dimensions={0} | all-to-all | bytes 15204352 | tf_op jit(solution)/shard_map/all_to_all | solution.py:42
  359.2 3.9 copy.29
  363.2 0.0 all-gather.2.cloned.1.call-update
  363.2 0.0 copy-start.1
  363.2 0.0 copy-start.2
  363.2 0.2 reduce-scatter.2.cloned.1.call-start
  363.5 272.5 %all-gather.2.cloned.1.call-done = bf16[3712,8192]{1,0:T(8,128)(2,1)} async-done(((bf16[464,8192]{1,0:T(8,128)(2,1)}), bf16[3712,8192]{1,0:T(8,128)(2,1)}) %all-gather.2.cloned.1.call-update) | async-done | bytes 60817424 | tf_op jit(solution)/shard_map/all_gather | solution.py:45
  635.9 0.0 copy-done
  635.9 26.3 %fusion.4 = bf16[128,8192]{0,1:T(8,128)(2,1)} fusion(bf16[3712,8192]{1,0:T(8,128)(2,1)} %all-gather.2.cloned.1.call-done, bf16[128,3712]{1,0:T(8,128)(2,1)S(1)} %copy-done), kind=kOutput, calls=%fused_computation.9 | convolution fusion | flops 7785676800 | bytes 63864832 | tf_op jit(solution)/shard_map/dot_general | solution.py:43
  662.2 0.0 reduce-scatter.2.cloned.1.call-update
  662.3 0.3 copy.24
  662.6 43.7 %reduce-scatter.2.cloned.1.call-done = bf16[128,2048]{0,1:T(8,128)(2,1)} async-done(((bf16[128,8192]{0,1:T(8,128)(2,1)}), bf16[128,2048]{0,1:T(8,128)(2,1)}) %reduce-scatter.2.cloned.1.call-update) | async-done | bytes 524304 | tf_op jit(solution)/shard_map/reduce_scatter | solution.py:48
  706.3 1.3 multiply_reduce_fusion
  707.6 9.9 %psum.15 = f32[128]{0:T(128)S(1)} all-reduce(f32[128]{0:T(128)S(1)} %multiply_reduce_fusion), channel_id=1, replica_groups=mesh['group'=4,'dp'=2,'tensor'=4] {'tensor'}, use_global_device_ids=true, to_apply=%region_4.0 | all-reduce | flops 128 | bytes 1024 | tf_op jit(solution)/shard_map/psum | solution.py:52
  717.5 1.4 fusion.5
  718.9 1.0 copy.27
  719.9 1.0 copy.28
  (4 shorter events, 0.0 us)
Async XLA Ops:
  7.2 628.8 %copy-start = (bf16[128,3712]{1,0:T(8,128)(2,1)S(1)}, bf16[128,3712]{1,0:T(8,128)(2,1)}, u32[]{:S(2)}) copy-start(bf16[128,3712]{1,0:T(8,128)(2,1)} %param.11) | copy-start | bytes 2850820
  7.2 628.7 %all-gather.2.cloned.1.call-start = ((), (), s32[]{:S(2)}) async-start(), calls=%async_computation.3 | async-start | bytes 68419584 | tf_op jit(solution)/shard_map/all_gather | solution.py:45
  363.2 299.1 %copy-start.1 = (bf16[128,2048]{1,0:T(8,128)(2,1)S(1)}, bf16[128,2048]{1,0:T(8,128)(2,1)}, u32[]{:S(2)}) copy-start(bf16[128,2048]{1,0:T(8,128)(2,1)} %param.12) | copy-start | bytes 1572868
  363.2 299.3 %copy-start.2 = (bf16[2048]{0:T(1024)(128)(2,1)S(1)}, bf16[2048]{0:T(1024)(128)(2,1)}, u32[]{:S(2)}) copy-start(bf16[2048]{0:T(1024)(128)(2,1)} %param.13) | copy-start | bytes 12292
  363.2 343.0 %reduce-scatter.2.cloned.1.call-start = ((), (), s32[]{:S(2)}) async-start(), calls=%async_computation.4 | async-start | bytes 2621440 | tf_op jit(solution)/shard_map/reduce_scatter | solution.py:48
Sparse Core Ops, SparseCore 0:
  363.3 272.5 all-gather.1
  662.4 43.8 reduce-scatter.1
where the time goes:
time: 728 us
  waiting for transfers between devices  316 us (43%)
  blocking collectives  313 us (43%)
  other arithmetic  46.5 us (6%)
  matrix products  26.3 us (4%)
  between operations  14.8 us (2%)
  local copies, waits for them, and re-layouts  10.2 us (1%)
    all_gather x1, waiting for transfers between devices, per_device(): lax.all_gather(received[0], ('group', 'dp'), axis=0, tiled=True)  272 us
    all_to_all x1, blocking collectives, per_device(): lax.all_to_all(arranged, ('dp', 'tensor'), split_axis=0, concat_axis=2, t...  173 us
    all_to_all x1, blocking collectives, per_device(): lax.all_to_all(pieces, 'group', split_axis=0, concat_axis=0, tiled=True)  88.7 us
    reduce_scatter x1, waiting for transfers between devices, per_device(): lax.psum_scatter(partial_value.astype(jnp.bfloat16), 'tensor', scatter_di...  43.7 us
    psum x1, blocking collectives, per_device(): lax.psum(jnp.sum(grad_float * grad_float), ('group', 'dp', 'tensor'))  42.2 us
    convert_element_type x1, other arithmetic, per_device(): shipped = weight_new.astype(jnp.bfloat16)  36 us
    dot_general x1, matrix products, per_device(): jnp.dot(hidden, lax.all_gather(received[0], ('group', 'dp'), axis=0, tile...  26.3 us
  transfers between devices with their start and end apart: 2, of which 2 were waited for; matrix products, arithmetic and copies ran while one was open for 0% of the time, Pallas kernels for 0%

commit v1 on v0

v1 whole, which is shorter than its diff:
```python
import math

import jax
import jax.numpy as jnp
from jax import lax
from jax.sharding import PartitionSpec as P

AXES = ("group", "dp", "tensor")

clip_rms = 0.5
beta_one = 0.9
beta_two = 0.95
bias_one = 1.0 - 0.9**10
bias_two = 1.0 - 0.95**10
adam_eps = 1e-08
learn_rate = 0.002


def permute(value, sizes, target):
    groups, ranks, slices = sizes
    index = lambda g, d, t: (g * ranks + d) * slices + t
    pairs = [
        (index(g, d, t), index(*target(g, d, t)))
        for g in range(groups)
        for d in range(ranks)
        for t in range(slices)
    ]
    return lax.ppermute(value, AXES, pairs)


def gather_hidden(hidden, sizes):
    groups, ranks, slices = sizes
    rows, units = hidden.shape
    split = slices // groups
    moved = permute(
        hidden, sizes, lambda g, d, t: (t // split, d, g * split + t % split)
    )
    full = lax.all_gather(moved, ("dp", "tensor"), axis=0, tiled=True)
    if split == 1:
        return full
    full = full.reshape(ranks * groups, split, rows, units).transpose(0, 2, 1, 3)
    return full.reshape(ranks * groups * rows, split * units)


def per_device(weight, moment, second, gradient, hidden, stream, norm_gain):
    sizes = tuple(lax.axis_size(axis) for axis in AXES)
    groups, ranks, slices = sizes
    g, d, t = (lax.axis_index(axis) for axis in AXES)
    entries = weight.size * groups * ranks * slices
    width = stream.shape[1] * slices
    rows = stream.shape[0]

    activations = gather_hidden(hidden, sizes)

    grad_float = gradient.astype(jnp.float32)
    grad_total = lax.psum(jnp.sum(grad_float * grad_float), AXES)
    factor = jnp.minimum(1.0, clip_rms * math.sqrt(entries) / (jnp.sqrt(grad_total) + 1e-06))
    clipped = factor * grad_float
    moment_new = beta_one * moment + (1.0 - beta_one) * clipped
    second_new = beta_two * second + (1.0 - beta_two) * clipped * clipped
    update = moment_new / bias_one / (jnp.sqrt(second_new / bias_two) + adam_eps)
    weight_new = weight - learn_rate * update
    shipped = weight_new.astype(jnp.bfloat16)

    term = jnp.dot(activations, shipped, preferred_element_type=jnp.float32)
    cols = term.shape[1]
    part = term.astype(jnp.bfloat16).reshape(ranks, groups, rows, cols)

    step = groups // 2
    while step >= 1:
        bit = (g // step) % 2
        pairs = part.reshape(ranks, 2, -1, rows, cols)
        kept = lax.dynamic_index_in_dim(pairs, bit, 1, keepdims=False)
        sent = lax.dynamic_index_in_dim(pairs, 1 - bit, 1, keepdims=False)
        got = permute(sent, sizes, lambda g, d, t, step=step: (g ^ step, d, t))
        part = (kept.astype(jnp.float32) + got.astype(jnp.float32)).astype(jnp.bfloat16)
        step //= 2
    part = part.reshape(ranks, rows, cols)

    place = (d * slices + t) % ranks
    summed = jnp.zeros((ranks, rows, cols), jnp.bfloat16)
    for turn in range(ranks):
        sent = lax.dynamic_index_in_dim(part, (place + turn) % ranks, 0, keepdims=False)

        def target(g, d, t, turn=turn):
            block = d * slices + t
            return (g, (block % ranks + turn) % ranks, block // ranks)

        got = permute(sent, sizes, target)
        summed = lax.dynamic_update_index_in_dim(summed, got, (d - turn) % ranks, 0)
    summed = summed.transpose(1, 0, 2).reshape(rows, ranks * cols)

    residual_sum = stream.astype(jnp.float32) + summed.astype(jnp.float32)
    squares = lax.psum(jnp.sum(residual_sum * residual_sum, axis=1), "tensor")
    normed = residual_sum * lax.rsqrt(squares / width + 1e-06)[:, None] * norm_gain.astype(jnp.float32)
    return (
        weight_new,
        moment_new,
        second_new,
        normed.astype(jnp.bfloat16),
        residual_sum.astype(jnp.bfloat16),
    )


def solution(mesh):
    master = P("group", ("dp", "tensor"))
    decode = P(("group", "dp"), "tensor")
    return jax.shard_map(
        per_device,
        mesh=mesh,
        in_specs=(master, master, master, master, decode, decode, P("tensor")),
        out_specs=(master, master, master, decode, decode),
        check_vma=False,
    )
```

time: 728 us -> 269 us (0.37)
  waiting for transfers between devices: 316 us -> 66.8 us
  blocking collectives: 313 us -> 107 us
  matrix products: 26.3 us -> 13.8 us
  starting transfers between devices: 0.26 us -> 8.6 us
    all_to_all x2 -> x0, blocking collectives: 261 us -> none  [the longest x1 173 us: per_device(): lax.all_to_all(arranged, ('dp', 'tensor'), split_axis=0, concat_axis=2, t...]
    all_gather x1, waiting for transfers between devices: 272 us -> 31.1 us  [gather_hidden(): full = lax.all_gather(moved, ('dp', 'tensor'), axis=0, tiled=True)]
    psum x1, blocking collectives: 42.2 us -> 88.7 us  [per_device(): grad_total = lax.psum(jnp.sum(grad_float * grad_float), AXES)]
    reduce_scatter x1 -> x0, waiting for transfers between devices: 43.7 us -> none  [per_device(): lax.psum_scatter(partial_value.astype(jnp.bfloat16), 'tensor', scatter_di...]
    ppermute x0 -> x5, waiting for transfers between devices: none -> 35.7 us  [permute(): return lax.ppermute(value, AXES, pairs)]
    sub x0 -> x1, other arithmetic: none -> 34.3 us  [per_device(): weight_new = weight - learn_rate * update]
    convert_element_type x1 -> x3, other arithmetic: 36 us -> 2.18 us  [the longest x2 1.82 us: per_device(): (kept.astype(jnp.float32) + got.astype(jnp.float32)).astype(jnp.bfloat16)]
    dot_general x1, matrix products: 26.3 us -> 13.8 us  [per_device(): term = jnp.dot(activations, shipped, preferred_element_type=jnp.float32)]
  transfers between devices with their start and end apart: 2 -> 6, of which waited for: 2 -> 4; matrix products, arithmetic and copies ran while one was open for 0% -> 16% of each run, Pallas kernels for 0% -> 0%
where the time goes in v1:
time: 269 us; the launch traced here: 268 us
  blocking collectives  107 us (40%)
  waiting for transfers between devices  66.8 us (25%)
  other arithmetic  47.6 us (18%)
  between operations  14.9 us (6%)
  matrix products  13.8 us (5%)
  local copies, waits for them, and re-layouts  9.65 us (4%)
  starting transfers between devices  8.6 us (3%)
    psum x1, blocking collectives, per_device(): grad_total = lax.psum(jnp.sum(grad_float * grad_float), AXES)  88.7 us
    ppermute x5, waiting for transfers between devices, permute(): return lax.ppermute(value, AXES, pairs)  35.7 us
    sub x1, other arithmetic, per_device(): weight_new = weight - learn_rate * update  34.3 us
    all_gather x1, waiting for transfers between devices, gather_hidden(): full = lax.all_gather(moved, ('dp', 'tensor'), axis=0, tiled=True)  31.1 us
    psum x1, blocking collectives, per_device(): squares = lax.psum(jnp.sum(residual_sum * residual_sum, axis=1), 'tensor')  18.3 us
    dot_general x1, matrix products, per_device(): term = jnp.dot(activations, shipped, preferred_element_type=jnp.float32)  13.8 us
    ppermute x5, starting transfers between devices, permute(): return lax.ppermute(value, AXES, pairs)  8.57 us
    reduce_sum x1, other arithmetic, per_device(): grad_total = lax.psum(jnp.sum(grad_float * grad_float), AXES)  7.67 us
  transfers between devices with their start and end apart: 6, of which 4 were waited for; matrix products, arithmetic and copies ran while one was open for 16% of the time, Pallas kernels for 0%

profile of v1, /device:TPU:0, one launch (start us, length us, event | category | flops | bytes accessed | tf_op | source)
XLA Modules:
  0.0 268.3 jit_solution(9306839919620196589)
XLA Ops:
  7.2 1.8 collective-permute-start
  9.1 1.0 copy-done
  10.1 7.7 %fusion.2 = f32[]{:T(128)} fusion(bf16[3712,1024]{1,0:T(8,128)(2,1)} %param.10), kind=kLoop, calls=%fused_computation.5 | loop fusion | flops 11403263 | bytes 7602180 | tf_op jit(solution)/shard_map/reduce_sum | solution.py:56
  17.7 88.7 %psum.14 = f32[]{:T(128)} all-reduce(f32[]{:T(128)} %fusion.2), channel_id=1, replica_groups=mesh['group'=4,'dp'=2,'tensor'=4] {'group','dp','tensor'}, use_global_device_ids=true, to_apply=%region_1.0 | all-reduce | flops 1 | bytes 8 | tf_op jit(solution)/shard_map/psum | solution.py:56
  107.1 34.3 %multiply_subtract_fusion = (f32[3712,1024]{1,0:T(8,128)}, f32[3712,1024]{1,0:T(8,128)}, f32[3712,1024]{1,0:T(8,128)}) fusion(f32[3712,1024]{1,0:T(8,128)} %param.7, bf16[3712,1024]{1,0:T(8,128)(2,1)} %param.10, f32[]{:T(128)S(6)} %min_shard_map.3, f32[3712,1024]{1,0:T(8,128)} %param.8, f32[3712,1024]{1,0:T(8,128)} %param.9), kind=kLoop, calls=%fused_computation.7 | loop fusion | flops 57016320 | bytes 98828288 | tf_op jit(solution)/shard_map/sub | solution.py:62
  141.4 31.1 %all-gather.2.cloned.1.call-done = bf16[1024,3712]{1,0:T(8,128)(2,1)} async-done(((bf16[128,3712]{1,0:T(8,128)(2,1)}), bf16[1024,3712]{1,0:T(8,128)(2,1)}) %all-gather.2.cloned.1.call-update) | async-done | bytes 7602192 | tf_op jit(solution)/shard_map/all_gather | solution.py:38
  172.5 13.8 %fusion.7 = bf16[1024,1024]{0,1:T(8,128)(2,1)S(1)} fusion(bf16[1024,3712]{1,0:T(8,128)(2,1)} %all-gather.2.cloned.1.call-done, f32[3712,1024]{1,0:T(8,128)} %get-tuple-element.5), kind=kOutput, calls=%fused_computation.12 | convolution fusion | flops 7789477888 | bytes 24903680 | tf_op jit(solution)/shard_map/dot_general | solution.py:65
  186.4 1.5 collective-permute-start.1
  187.9 23.1 %collective-permute-done.1 = bf16[2,2,128,1024]{3,2,1,0:T(8,128)(2,1)} collective-permute-done((bf16[2,2,128,1024]{3,2,1,0:T(8,128)(2,1)S(1)}, bf16[2,2,128,1024]{3,2,1,0:T(8,128)(2,1)}, u32[]{:S(2)}, u32[]{:S(2)}) %collective-permute-start.1) | collective-permute-done | bytes 1048608 | tf_op jit(solution)/shard_map/ppermute | solution.py:28
  211.1 1.6 fusion.6
  212.9 1.8 collective-permute-done.2
  215.0 0.7 collective-permute-start.3
  215.7 4.4 %collective-permute-start.4 = (bf16[128,1024]{1,0:T(8,128)(2,1)S(1)}, bf16[128,1024]{1,0:T(8,128)(2,1)S(1)}, u32[]{:S(2)}, u32[]{:S(2)}) collective-permute-start(bf16[128,1024]{1,0:T(8,128)(2,1)S(1)} %get-tuple-element.10), channel_id=1, source_target_pairs={{0,4},{1,0},{2,5},{3,1},{4,6},{5,2},{6,7},{7,3},{8,12},{9,8},{10,1... | collective-permute-start | bytes 786440 | tf_op jit(solution)/shard_map/ppermute | solution.py:28
  220.1 0.4 copy.12
  220.5 10.7 %collective-permute-done.4 = bf16[128,1024]{1,0:T(8,128)(2,1)S(1)} collective-permute-done((bf16[128,1024]{1,0:T(8,128)(2,1)S(1)}, bf16[128,1024]{1,0:T(8,128)(2,1)S(1)}, u32[]{:S(2)}, u32[]{:S(2)}) %collective-permute-start.4) | collective-permute-done | bytes 262176 | tf_op jit(solution)/shard_map/ppermute | solution.py:28
  231.2 0.4 copy.13
  231.6 0.3 broadcast_in_dim.12
  231.9 3.5 %dynamic_update_slice.7 = bf16[2,128,1024]{2,0,1:T(2,128)(2,1)S(1)} dynamic-update-slice(bf16[2,128,1024]{2,0,1:T(2,128)(2,1)S(1)} %broadcast_in_dim.12, bf16[1,128,1024]{2,0,1:T(2,128)(2,1)S(1)} %copy.12, s32[]{:T(128)S(6)} %select_n.75, s32[]{:T(128)} %constant.123.clone.1, s32[]{:T(128)} %constant.123.clone.1) | dynamic-update-slice | bytes 524292 | tf_op jit(solution)/shard_map/jit(dynamic_update_index_in_dim)/dynamic_update_slice | solution.py:90
  235.5 3.5 %dynamic_update_slice.8 = bf16[2,128,1024]{2,0,1:T(2,128)(2,1)S(1)} dynamic-update-slice(bf16[2,128,1024]{2,0,1:T(2,128)(2,1)S(1)} %dynamic_update_slice.7, bf16[1,128,1024]{2,0,1:T(2,128)(2,1)S(1)} %copy.13, s32[]{:T(128)S(6)} %select_n.79, s32[]{:T(128)} %constant.123.clone.1, s32[]{:T(128)} %constant.123.clone.1) | dynamic-update-slice | bytes 524292 | tf_op jit(solution)/shard_map/jit(dynamic_update_index_in_dim)/dynamic_update_slice | solution.py:90
  239.0 0.4 convert_element_type.76
  239.4 0.3 copy.14
  239.7 1.3 multiply_reduce_fusion
  241.0 18.3 %psum.15 = f32[128]{0:T(128)S(1)} all-reduce(f32[128]{0:T(128)S(1)} %multiply_reduce_fusion), channel_id=1, replica_groups=mesh['group'=4,'dp'=2,'tensor'=4] {'tensor'}, use_global_device_ids=true, to_apply=%region_3.4 | all-reduce | flops 128 | bytes 1024 | tf_op jit(solution)/shard_map/psum | solution.py:94
  259.3 2.2 fusion.10
  (14 shorter events, 0.5 us)
Async XLA Ops:
  7.2 165.3 %all-gather.2.cloned.1.call-start = ((), (), s32[]{:S(2)}) async-start(), calls=%async_computation | async-start | bytes 8552448 | tf_op jit(solution)/shard_map/all_gather | solution.py:38
  7.2 1.9 collective-permute-start
  9.1 1.0 copy-start
  172.5 47.6 %copy-start.1 = (bf16[2048]{0:T(1024)(128)(2,1)S(1)}, bf16[2048]{0:T(1024)(128)(2,1)}, u32[]{:S(2)}) copy-start(bf16[2048]{0:T(1024)(128)(2,1)} %param.13) | copy-start | bytes 12292
  186.4 24.7 %collective-permute-start.1 = (bf16[2,2,128,1024]{3,2,1,0:T(8,128)(2,1)S(1)}, bf16[2,2,128,1024]{3,2,1,0:T(8,128)(2,1)}, u32[]{:S(2)}, u32[]{:S(2)}) collective-permute-start(bf16[2,2,128,1024]{3,2,1,0:T(8,128)(2,1)S(1)} %dynamic-slice_bitcast_fusion), channel_id=1, source_target_pairs={{0,16},{1,17},{2,18},{3,19},{4,20},{5,21},{6,22},{7,23},{8,24},{9,... | collective-permute-start | bytes 3145736 | tf_op jit(solution)/shard_map/ppermute | solution.py:28
  212.7 2.0 collective-permute-start.2
  215.0 5.1 %collective-permute-start.3 = (bf16[128,1024]{1,0:T(8,128)(2,1)S(1)}, bf16[128,1024]{1,0:T(8,128)(2,1)S(1)}, u32[]{:S(2)}, u32[]{:S(2)}) collective-permute-start(bf16[128,1024]{1,0:T(8,128)(2,1)S(1)} %get-tuple-element.11), channel_id=1, source_target_pairs={{0,0},{1,4},{2,1},{3,5},{4,2},{5,6},{6,3},{7,7},{8,8},{9,12},{10,9... | collective-permute-start | bytes 786440 | tf_op jit(solution)/shard_map/ppermute | solution.py:28
  215.7 15.6 %collective-permute-start.4 = (bf16[128,1024]{1,0:T(8,128)(2,1)S(1)}, bf16[128,1024]{1,0:T(8,128)(2,1)S(1)}, u32[]{:S(2)}, u32[]{:S(2)}) collective-permute-start(bf16[128,1024]{1,0:T(8,128)(2,1)S(1)} %get-tuple-element.10), channel_id=1, source_target_pairs={{0,4},{1,0},{2,5},{3,1},{4,6},{5,2},{6,7},{7,3},{8,12},{9,8},{10,1... | collective-permute-start | bytes 786440 | tf_op jit(solution)/shard_map/ppermute | solution.py:28
Sparse Core Ops, SparseCore 0:
  10.2 162.2 all-gather.1

commit v2 on v1

v2 whole, which is shorter than its diff:
```python
import math

import jax
import jax.numpy as jnp
from jax import lax
from jax.sharding import PartitionSpec as P

AXES = ("group", "dp", "tensor")

clip_rms = 0.5
beta_one = 0.9
beta_two = 0.95
bias_one = 1.0 - 0.9**10
bias_two = 1.0 - 0.95**10
adam_eps = 1e-08
learn_rate = 0.002


def permute(value, sizes, target):
    groups, ranks, slices = sizes
    index = lambda g, d, t: (g * ranks + d) * slices + t
    pairs = [
        (index(g, d, t), index(*target(g, d, t)))
        for g in range(groups)
        for d in range(ranks)
        for t in range(slices)
    ]
    return lax.ppermute(value, AXES, pairs)


def total_over(value, sizes, axes):
    groups, ranks, slices = sizes
    if slices != groups:
        return lax.psum(value, axes)
    total = value
    for k in range(1, slices):
        total = total + permute(value, sizes, lambda g, d, t, k=k: (g, d, (t + k) % slices))
    if axes == "tensor":
        return total
    line = total
    for k in range(1, groups * ranks):

        def target(g, d, t, k=k):
            place = (g * ranks + d + k) % (groups * ranks)
            return (place // ranks, place % ranks, t)

        total = total + permute(line, sizes, target)
    return total


def per_device(weight, moment, second, gradient, hidden, stream, norm_gain):
    sizes = tuple(lax.axis_size(axis) for axis in AXES)
    groups, ranks, slices = sizes
    g, d, t = (lax.axis_index(axis) for axis in AXES)
    entries = weight.size * groups * ranks * slices
    width = stream.shape[1] * slices
    rows, units = hidden.shape
    split = slices // groups
    pick = lambda value, place: lax.dynamic_index_in_dim(value, place, 0, keepdims=False)

    moved = permute(
        hidden, sizes, lambda g, d, t: (t // split, d, g * split + t % split)
    )
    if split == 1:
        near = [moved] + [
            permute(moved, sizes, lambda g, d, t, k=k: (g, d, (t + k) % slices))
            for k in range(1, slices)
        ]

    grad_float = gradient.astype(jnp.float32)
    squared = jnp.full((1, 128), jnp.sum(grad_float * grad_float))
    grad_total = total_over(squared, sizes, AXES)[0, 0]
    factor = jnp.minimum(1.0, clip_rms * math.sqrt(entries) / (jnp.sqrt(grad_total) + 1e-06))
    if split == 1:
        factor, *far = lax.optimization_barrier((factor, *near[1:]))
        near = [moved, *far]
    clipped = factor * grad_float
    moment_new = beta_one * moment + (1.0 - beta_one) * clipped
    second_new = beta_two * second + (1.0 - beta_two) * clipped * clipped
    update = moment_new / bias_one / (jnp.sqrt(second_new / bias_two) + adam_eps)
    weight_new = weight - learn_rate * update
    shipped = weight_new.astype(jnp.bfloat16)
    cols = shipped.shape[1]

    if split == 1:
        lots = [jnp.concatenate(near, axis=0)]
        for r in range(1, ranks):
            far = [
                permute(piece, sizes, lambda g, d, t, r=r: (g, (d + r) % ranks, t))
                for piece in near
            ]
            lots.append(jnp.concatenate(far, axis=0))
    else:
        full = lax.all_gather(moved, ("dp", "tensor"), axis=0, tiled=True)
        full = full.reshape(ranks, groups, split, rows, units).transpose(0, 1, 3, 2, 4)
        full = full.reshape(ranks, groups * rows, split * units)
        lots = [pick(full, (d - r) % ranks) for r in range(ranks)]

    sums = []
    for lot in lots:
        term = jnp.dot(lot, shipped, preferred_element_type=jnp.float32)
        part = term.astype(jnp.bfloat16).reshape(groups, rows, cols)
        if split == 1:
            part = jnp.stack([pick(part, (t - place) % groups) for place in range(groups)])
        step = 1
        while step < groups:
            bit = (g // step) % 2
            pairs = part.reshape(-1, 2, rows, cols)
            kept = lax.dynamic_index_in_dim(pairs, bit, 1, keepdims=False)
            sent = lax.dynamic_index_in_dim(pairs, 1 - bit, 1, keepdims=False)
            got = permute(sent, sizes, lambda g, d, t, step=step: (g ^ step, d, t))
            part = (kept.astype(jnp.float32) + got.astype(jnp.float32)).astype(jnp.bfloat16)
            step *= 2
        sums.append(part.reshape(rows, cols))
    sums = jnp.stack(sums)

    place = (d * slices + t) % ranks
    arrived = []
    for turn in range(ranks):

        def target(g, d, t, turn=turn):
            block = d * slices + t
            return (g, (block % ranks + turn) % ranks, block // ranks)

        arrived.append(permute(pick(sums, (d - place - turn) % ranks), sizes, target))
    arrived = jnp.stack(arrived)
    summed = jnp.concatenate([pick(arrived, (d - h) % ranks) for h in range(ranks)], axis=1)

    residual_sum = stream.astype(jnp.float32) + summed.astype(jnp.float32)
    squares = total_over(jnp.sum(residual_sum * residual_sum, axis=1), sizes, "tensor")
    normed = residual_sum * lax.rsqrt(squares / width + 1e-06)[:, None] * norm_gain.astype(jnp.float32)
    return (
        weight_new,
        moment_new,
        second_new,
        normed.astype(jnp.bfloat16),
        residual_sum.astype(jnp.bfloat16),
    )


def solution(mesh):
    master = P("group", ("dp", "tensor"))
    decode = P(("group", "dp"), "tensor")
    return jax.shard_map(
        per_device,
        mesh=mesh,
        in_specs=(master, master, master, master, decode, decode, P("tensor")),
        out_specs=(master, master, master, decode, decode),
        check_vma=False,
    )
```

time: 269 us -> 316 us (1.17)
  blocking collectives: 107 us -> 0 us
  starting transfers between devices: 8.6 us -> 107 us
  waiting for transfers between devices: 66.8 us -> 140 us
  between operations: 14.9 us -> 0.99 us
  local copies, waits for them, and re-layouts: 9.65 us -> 3.03 us
  matrix products: 13.8 us -> 18.1 us
    psum x2 -> x0, blocking collectives: 107 us -> none  [the longest x1 88.7 us: per_device(): grad_total = lax.psum(jnp.sum(grad_float * grad_float), AXES)]
    ppermute x5 -> x27, waiting for transfers between devices: 35.7 us -> 140 us  [permute(): return lax.ppermute(value, AXES, pairs)]
    ppermute x5 -> x27, starting transfers between devices: 8.57 us -> 107 us  [permute(): return lax.ppermute(value, AXES, pairs)]
    all_gather x1 -> x0, waiting for transfers between devices: 31.1 us -> none  [gather_hidden(): full = lax.all_gather(moved, ('dp', 'tensor'), axis=0, tiled=True)]
    dynamic_update_slice x2 -> x0, local copies, waits for them, and re-layouts: 7.07 us -> none  [per_device(): summed = lax.dynamic_update_index_in_dim(summed, got, (d - turn) % ranks, 0)]
    dot_general x1 -> x2, matrix products: 13.8 us -> 18.1 us  [per_device(): term = jnp.dot(lot, shipped, preferred_element_type=jnp.float32)]
  transfers between devices with their start and end apart: 6 -> 27, of which waited for: 4 -> 15; matrix products, arithmetic and copies ran while one was open for 16% -> 18% of each run, Pallas kernels for 0% -> 0%
where the time goes in v2:
time: 316 us
  waiting for transfers between devices  140 us (44%)
  starting transfers between devices  107 us (34%)
  other arithmetic  47 us (15%)
  matrix products  18.1 us (6%)
    ppermute x27, waiting for transfers between devices, permute(): return lax.ppermute(value, AXES, pairs)  140 us
    ppermute x27, starting transfers between devices, permute(): return lax.ppermute(value, AXES, pairs)  107 us
    sub x1, other arithmetic, per_device(): weight_new = weight - learn_rate * update  33.9 us
    dot_general x2, matrix products, per_device(): term = jnp.dot(lot, shipped, preferred_element_type=jnp.float32)  18.1 us
    reduce_sum x1, other arithmetic, per_device(): squared = jnp.full((1, 128), jnp.sum(grad_float * grad_float))  7.67 us
  transfers between devices with their start and end apart: 27, of which 15 were waited for; matrix products, arithmetic and copies ran while one was open for 18% of the time, Pallas kernels for 0%

profile of v2, /device:TPU:0, one launch (start us, length us, event | category | flops | bytes accessed | tf_op | source)
XLA Modules:
  0.0 315.8 jit_solution(8065940846771369089)
XLA Ops:
  2.5 22.1 %collective-permute-start.11 = (bf16[128,3712]{1,0:T(8,128)(2,1)S(1)}, bf16[128,3712]{1,0:T(8,128)(2,1)}, u32[]{:S(2)}, u32[]{:S(2)}) collective-permute-start(bf16[128,3712]{1,0:T(8,128)(2,1)S(1)} %collective-permute-done.10), channel_id=1, source_target_pairs={{0,1},{1,2},{2,3},{3,0},{4,5},{5,6},{6,7},{7,4},{8,9},{9,10},{10,1... | collective-permute-start | bytes 2850824 | tf_op jit(solution)/shard_map/ppermute | solution.py:28
  24.5 45.3 %collective-permute-start.12 = (bf16[128,3712]{1,0:T(8,128)(2,1)S(1)}, bf16[128,3712]{1,0:T(8,128)(2,1)}, u32[]{:S(2)}, u32[]{:S(2)}) collective-permute-start(bf16[128,3712]{1,0:T(8,128)(2,1)S(1)} %collective-permute-done.10), channel_id=1, source_target_pairs={{0,2},{1,3},{2,0},{3,1},{4,6},{5,7},{6,4},{7,5},{8,10},{9,11},{10,... | collective-permute-start | bytes 2850824 | tf_op jit(solution)/shard_map/ppermute | solution.py:28
  69.9 2.9 collective-permute-start.13
  72.8 7.7 %fusion.2 = f32[]{:T(128)} fusion(bf16[3712,1024]{1,0:T(8,128)(2,1)} %param.10), kind=kLoop, calls=%fused_computation.5 | loop fusion | flops 11403263 | bytes 7602180 | tf_op jit(solution)/shard_map/reduce_sum | solution.py:71
  81.7 31.9 %collective-permute-done = f32[1,128]{1,0:T(1,128)S(1)} collective-permute-done((f32[1,128]{1,0:T(1,128)S(1)}, f32[1,128]{1,0:T(1,128)S(1)}, u32[]{:S(2)}, u32[]{:S(2)}) %collective-permute-start) | collective-permute-done | bytes 544 | tf_op jit(solution)/shard_map/ppermute | solution.py:28
  113.6 18.0 %collective-permute-done.1 = f32[1,128]{1,0:T(1,128)S(1)} collective-permute-done((f32[1,128]{1,0:T(1,128)S(1)}, f32[1,128]{1,0:T(1,128)S(1)}, u32[]{:S(2)}, u32[]{:S(2)}) %collective-permute-start.1) | collective-permute-done | bytes 544 | tf_op jit(solution)/shard_map/ppermute | solution.py:28
  131.6 21.8 %collective-permute-done.2 = f32[1,128]{1,0:T(1,128)S(1)} collective-permute-done((f32[1,128]{1,0:T(1,128)S(1)}, f32[1,128]{1,0:T(1,128)S(1)}, u32[]{:S(2)}, u32[]{:S(2)}) %collective-permute-start.2) | collective-permute-done | bytes 544 | tf_op jit(solution)/shard_map/ppermute | solution.py:28
  155.6 2.3 collective-permute-done.3
  158.5 3.8 %collective-permute-done.5 = f32[1,128]{1,0:T(1,128)S(1)} collective-permute-done((f32[1,128]{1,0:T(1,128)S(1)}, f32[1,128]{1,0:T(1,128)S(1)}, u32[]{:S(2)}, u32[]{:S(2)}) %collective-permute-start.5) | collective-permute-done | bytes 544 | tf_op jit(solution)/shard_map/ppermute | solution.py:28
  162.7 2.6 collective-permute-done.7
  165.3 3.6 %collective-permute-done.9 = f32[1,128]{1,0:T(1,128)S(1)} collective-permute-done((f32[1,128]{1,0:T(1,128)S(1)}, f32[1,128]{1,0:T(1,128)S(1)}, u32[]{:S(2)}, u32[]{:S(2)}) %collective-permute-start.9) | collective-permute-done | bytes 544 | tf_op jit(solution)/shard_map/ppermute | solution.py:28
  173.3 33.9 %multiply_subtract_fusion = (f32[3712,1024]{1,0:T(8,128)}, f32[3712,1024]{1,0:T(8,128)}, f32[3712,1024]{1,0:T(8,128)}) fusion(f32[3712,1024]{1,0:T(8,128)} %param.7, bf16[3712,1024]{1,0:T(8,128)(2,1)} %param.10, f32[]{:T(128)} %bitcast, f32[3712,1024]{1,0:T(8,128)} %param.8, f32[3712,1024]{1,0:T(8,128)} %param.9), kind=kLoop, calls=%fused_computation.7 | loop fusion | flops 57016320 | bytes 98828288 | tf_op jit(solution)/shard_map/sub | solution.py:81
  207.2 10.6 %fusion.27 = bf16[512,1024]{1,0:T(8,128)(2,1)S(1)} fusion(f32[3712,1024]{1,0:T(8,128)} %get-tuple-element.13, bf16[128,3712]{1,0:T(8,128)(2,1)} %collective-permute-done.13, bf16[128,3712]{1,0:T(8,128)(2,1)} %collective-permute-done.12, bf16[128,3712]{1,0:T(8,128)(2,1)} %collective-permute-done.11, bf16[128,3712]{1,0:T(8,128)(2,1)S(1)} %collective-permute-done.10), kind=kOutput, calls=%fused_computation.27 | convolution fusion | flops 3911843840 | bytes 20054016 | tf_op jit(solution)/shard_map/dot_general | solution.py:101
  217.9 16.1 %collective-permute-done.18 = bf16[128,3712]{1,0:T(8,128)(2,1)} collective-permute-done((bf16[128,3712]{1,0:T(8,128)(2,1)}, bf16[128,3712]{1,0:T(8,128)(2,1)}, u32[]{:S(2)}, u32[]{:S(2)}) %collective-permute-start.18) | collective-permute-done | bytes 950304 | tf_op jit(solution)/shard_map/ppermute | solution.py:28
  234.0 18.7 %collective-permute-done.19 = bf16[128,3712]{1,0:T(8,128)(2,1)} collective-permute-done((bf16[128,3712]{1,0:T(8,128)(2,1)}, bf16[128,3712]{1,0:T(8,128)(2,1)}, u32[]{:S(2)}, u32[]{:S(2)}) %collective-permute-start.19) | collective-permute-done | bytes 950304 | tf_op jit(solution)/shard_map/ppermute | solution.py:28
  252.6 7.4 %fusion.22 = bf16[512,1024]{1,0:T(8,128)(2,1)} fusion(f32[3712,1024]{1,0:T(8,128)S(1)} %bitcast.29, bf16[128,3712]{1,0:T(8,128)(2,1)} %collective-permute-done.19, bf16[128,3712]{1,0:T(8,128)(2,1)} %collective-permute-done.18, bf16[128,3712]{1,0:T(8,128)(2,1)} %collective-permute-done.17, bf16[128,3712]{1,0:T(8,128)(2,1)} %collective-permute-done.16), kind=kOutput, calls=%fused_computation.26 | convolution fusion | flops 3911843840 | bytes 20054016 | tf_op jit(solution)/shard_map/dot_general | solution.py:101
  266.6 1.9 collective-permute-start.15
  268.5 5.8 %collective-permute-done.21 = bf16[1,128,1024]{2,1,0:T(8,128)(2,1)S(1)} collective-permute-done((bf16[1,128,1024]{2,1,0:T(8,128)(2,1)S(1)}, bf16[1,128,1024]{2,1,0:T(8,128)(2,1)S(1)}, u32[]{:S(2)}, u32[]{:S(2)}) %collective-permute-start.21) | collective-permute-done | bytes 262176 | tf_op jit(solution)/shard_map/ppermute | solution.py:28
  274.4 4.7 %collective-permute-done.15 = bf16[1,128,1024]{2,1,0:T(8,128)(2,1)S(1)} collective-permute-done((bf16[1,128,1024]{2,1,0:T(8,128)(2,1)S(1)}, bf16[1,128,1024]{2,1,0:T(8,128)(2,1)S(1)}, u32[]{:S(2)}, u32[]{:S(2)}) %collective-permute-start.15) | collective-permute-done | bytes 262176 | tf_op jit(solution)/shard_map/ppermute | solution.py:28
  280.1 6.6 %collective-permute-start.23 = (bf16[128,1024]{1,0:T(8,128)(2,1)S(1)}, bf16[128,1024]{1,0:T(8,128)(2,1)S(1)}, u32[]{:S(2)}, u32[]{:S(2)}) collective-permute-start(bf16[128,1024]{1,0:T(8,128)(2,1)S(1)} %get-tuple-element.28), channel_id=1, source_target_pairs={{0,4},{1,0},{2,5},{3,1},{4,6},{5,2},{6,7},{7,3},{8,12},{9,8},{10,1... | collective-permute-start | bytes 786440 | tf_op jit(solution)/shard_map/ppermute | solution.py:28
  286.7 8.4 %collective-permute-done.23 = bf16[128,1024]{1,0:T(8,128)(2,1)S(1)} collective-permute-done((bf16[128,1024]{1,0:T(8,128)(2,1)S(1)}, bf16[128,1024]{1,0:T(8,128)(2,1)S(1)}, u32[]{:S(2)}, u32[]{:S(2)}) %collective-permute-start.23) | collective-permute-done | bytes 262176 | tf_op jit(solution)/shard_map/ppermute | solution.py:28
  295.6 8.7 %collective-permute-start.24 = (f32[128]{0:T(128)S(1)}, f32[128]{0:T(128)S(1)}, u32[]{:S(2)}, u32[]{:S(2)}) collective-permute-start(f32[128]{0:T(128)S(1)} %multiply_reduce_fusion), channel_id=1, source_target_pairs={{0,1},{1,2},{2,3},{3,0},{4,5},{5,6},{6,7},{7,4},{8,9},{9,10},{10,1... | collective-permute-start | bytes 1544 | tf_op jit(solution)/shard_map/ppermute | solution.py:28
  304.3 6.1 %collective-permute-start.25 = (f32[128]{0:T(128)S(1)}, f32[128]{0:T(128)S(1)}, u32[]{:S(2)}, u32[]{:S(2)}) collective-permute-start(f32[128]{0:T(128)S(1)} %multiply_reduce_fusion), channel_id=1, source_target_pairs={{0,2},{1,3},{2,0},{3,1},{4,6},{5,7},{6,4},{7,5},{8,10},{9,11},{10,... | collective-permute-start | bytes 1544 | tf_op jit(solution)/shard_map/ppermute | solution.py:28
  310.4 2.8 collective-permute-start.26
  (67 shorter events, 21.0 us)
Async XLA Ops:
  2.5 168.1 %collective-permute-start.11 = (bf16[128,3712]{1,0:T(8,128)(2,1)S(1)}, bf16[128,3712]{1,0:T(8,128)(2,1)}, u32[]{:S(2)}, u32[]{:S(2)}) collective-permute-start(bf16[128,3712]{1,0:T(8,128)(2,1)S(1)} %collective-permute-done.10), channel_id=1, source_target_pairs={{0,1},{1,2},{2,3},{3,0},{4,5},{5,6},{6,7},{7,4},{8,9},{9,10},{10,1... | collective-permute-start | bytes 2850824 | tf_op jit(solution)/shard_map/ppermute | solution.py:28
  24.5 146.0 %collective-permute-start.12 = (bf16[128,3712]{1,0:T(8,128)(2,1)S(1)}, bf16[128,3712]{1,0:T(8,128)(2,1)}, u32[]{:S(2)}, u32[]{:S(2)}) collective-permute-start(bf16[128,3712]{1,0:T(8,128)(2,1)S(1)} %collective-permute-done.10), channel_id=1, source_target_pairs={{0,2},{1,3},{2,0},{3,1},{4,6},{5,7},{6,4},{7,5},{8,10},{9,11},{10,... | collective-permute-start | bytes 2850824 | tf_op jit(solution)/shard_map/ppermute | solution.py:28
  69.9 100.7 %collective-permute-start.13 = (bf16[128,3712]{1,0:T(8,128)(2,1)S(1)}, bf16[128,3712]{1,0:T(8,128)(2,1)}, u32[]{:S(2)}, u32[]{:S(2)}) collective-permute-start(bf16[128,3712]{1,0:T(8,128)(2,1)S(1)} %collective-permute-done.10), channel_id=1, source_target_pairs={{0,3},{1,0},{2,1},{3,2},{4,7},{5,4},{6,5},{7,6},{8,11},{9,8},{10,9... | collective-permute-start | bytes 2850824 | tf_op jit(solution)/shard_map/ppermute | solution.py:28
  81.1 32.5 %collective-permute-start = (f32[1,128]{1,0:T(1,128)S(1)}, f32[1,128]{1,0:T(1,128)S(1)}, u32[]{:S(2)}, u32[]{:S(2)}) collective-permute-start(f32[1,128]{1,0:T(1,128)S(1)} %broadcast_in_dim.2), channel_id=1, source_target_pairs={{0,1},{1,2},{2,3},{3,0},{4,5},{5,6},{6,7},{7,4},{8,9},{9,10},{10,1... | collective-permute-start | bytes 1544 | tf_op jit(solution)/shard_map/ppermute | solution.py:28
  81.2 50.4 %collective-permute-start.1 = (f32[1,128]{1,0:T(1,128)S(1)}, f32[1,128]{1,0:T(1,128)S(1)}, u32[]{:S(2)}, u32[]{:S(2)}) collective-permute-start(f32[1,128]{1,0:T(1,128)S(1)} %broadcast_in_dim.2), channel_id=1, source_target_pairs={{0,2},{1,3},{2,0},{3,1},{4,6},{5,7},{6,4},{7,5},{8,10},{9,11},{10,... | collective-permute-start | bytes 1544 | tf_op jit(solution)/shard_map/ppermute | solution.py:28
  113.6 39.7 %collective-permute-start.2 = (f32[1,128]{1,0:T(1,128)S(1)}, f32[1,128]{1,0:T(1,128)S(1)}, u32[]{:S(2)}, u32[]{:S(2)}) collective-permute-start(f32[1,128]{1,0:T(1,128)S(1)} %broadcast_in_dim.2), channel_id=1, source_target_pairs={{0,3},{1,0},{2,1},{3,2},{4,7},{5,4},{6,5},{7,6},{8,11},{9,8},{10,9... | collective-permute-start | bytes 1544 | tf_op jit(solution)/shard_map/ppermute | solution.py:28
  154.0 3.9 %collective-permute-start.3 = (f32[1,128]{1,0:T(1,128)S(1)}, f32[1,128]{1,0:T(1,128)S(1)}, u32[]{:S(2)}, u32[]{:S(2)}) collective-permute-start(f32[1,128]{1,0:T(1,128)S(1)} %add_add_fusion.1), channel_id=1, source_target_pairs={{0,4},{1,5},{2,6},{3,7},{4,8},{5,9},{6,10},{7,11},{8,12},{9,13},{1... | collective-permute-start | bytes 1544 | tf_op jit(solution)/shard_map/ppermute | solution.py:28
  155.6 3.0 collective-permute-start.4
  157.9 4.4 %collective-permute-start.5 = (f32[1,128]{1,0:T(1,128)S(1)}, f32[1,128]{1,0:T(1,128)S(1)}, u32[]{:S(2)}, u32[]{:S(2)}) collective-permute-start(f32[1,128]{1,0:T(1,128)S(1)} %add_add_fusion.1), channel_id=1, source_target_pairs={{0,12},{1,13},{2,14},{3,15},{4,16},{5,17},{6,18},{7,19},{8,20},{9,... | collective-permute-start | bytes 1544 | tf_op jit(solution)/shard_map/ppermute | solution.py:28
  158.5 3.8 %collective-permute-start.6 = (f32[1,128]{1,0:T(1,128)S(1)}, f32[1,128]{1,0:T(1,128)S(1)}, u32[]{:S(2)}, u32[]{:S(2)}) collective-permute-start(f32[1,128]{1,0:T(1,128)S(1)} %add_add_fusion.1), channel_id=1, source_target_pairs={{0,16},{1,17},{2,18},{3,19},{4,20},{5,21},{6,22},{7,23},{8,24},{9,... | collective-permute-start | bytes 1544 | tf_op jit(solution)/shard_map/ppermute | solution.py:28
  162.4 3.0 collective-permute-start.7
  162.4 3.0 collective-permute-start.8
  165.3 3.6 %collective-permute-start.9 = (f32[1,128]{1,0:T(1,128)S(1)}, f32[1,128]{1,0:T(1,128)S(1)}, u32[]{:S(2)}, u32[]{:S(2)}) collective-permute-start(f32[1,128]{1,0:T(1,128)S(1)} %add_add_fusion.1), channel_id=1, source_target_pairs={{0,28},{1,29},{2,30},{3,31},{4,0},{5,1},{6,2},{7,3},{8,4},{9,5},{1... | collective-permute-start | bytes 1544 | tf_op jit(solution)/shard_map/ppermute | solution.py:28
  169.1 48.8 %collective-permute-start.16 = (bf16[128,3712]{1,0:T(8,128)(2,1)S(1)}, bf16[128,3712]{1,0:T(8,128)(2,1)}, u32[]{:S(2)}, u32[]{:S(2)}) collective-permute-start(bf16[128,3712]{1,0:T(8,128)(2,1)S(1)} %collective-permute-done.10), channel_id=1, source_target_pairs={{0,4},{1,5},{2,6},{3,7},{4,0},{5,1},{6,2},{7,3},{8,12},{9,13},{10,... | collective-permute-start | bytes 2850824 | tf_op jit(solution)/shard_map/ppermute | solution.py:28
  170.6 47.3 %collective-permute-start.17 = (bf16[128,3712]{1,0:T(8,128)(2,1)}, bf16[128,3712]{1,0:T(8,128)(2,1)}, u32[]{:S(2)}, u32[]{:S(2)}) collective-permute-start(bf16[128,3712]{1,0:T(8,128)(2,1)} %collective-permute-done.11), channel_id=1, source_target_pairs={{0,4},{1,5},{2,6},{3,7},{4,0},{5,1},{6,2},{7,3},{8,12},{9,13},{10,... | collective-permute-start | bytes 2850824 | tf_op jit(solution)/shard_map/ppermute | solution.py:28
  171.2 62.7 %collective-permute-start.18 = (bf16[128,3712]{1,0:T(8,128)(2,1)}, bf16[128,3712]{1,0:T(8,128)(2,1)}, u32[]{:S(2)}, u32[]{:S(2)}) collective-permute-start(bf16[128,3712]{1,0:T(8,128)(2,1)} %collective-permute-done.12), channel_id=1, source_target_pairs={{0,4},{1,5},{2,6},{3,7},{4,0},{5,1},{6,2},{7,3},{8,12},{9,13},{10,... | collective-permute-start | bytes 2850824 | tf_op jit(solution)/shard_map/ppermute | solution.py:28
  172.7 79.9 %collective-permute-start.19 = (bf16[128,3712]{1,0:T(8,128)(2,1)}, bf16[128,3712]{1,0:T(8,128)(2,1)}, u32[]{:S(2)}, u32[]{:S(2)}) collective-permute-start(bf16[128,3712]{1,0:T(8,128)(2,1)} %collective-permute-done.13), channel_id=1, source_target_pairs={{0,4},{1,5},{2,6},{3,7},{4,0},{5,1},{6,2},{7,3},{8,12},{9,13},{10,... | collective-permute-start | bytes 2850824 | tf_op jit(solution)/shard_map/ppermute | solution.py:28
  265.1 9.2 %collective-permute-start.21 = (bf16[1,128,1024]{2,1,0:T(8,128)(2,1)S(1)}, bf16[1,128,1024]{2,1,0:T(8,128)(2,1)S(1)}, u32[]{:S(2)}, u32[]{:S(2)}) collective-permute-start(bf16[1,128,1024]{2,1,0:T(8,128)(2,1)S(1)} %constant_dynamic-slice_fusion), channel_id=1, source_target_pairs={{0,16},{1,17},{2,18},{3,19},{4,20},{5,21},{6,22},{7,23},{8,24},{9,... | collective-permute-start | bytes 786440 | tf_op jit(solution)/shard_map/ppermute | solution.py:28
  266.6 12.5 %collective-permute-start.15 = (bf16[1,128,1024]{2,1,0:T(8,128)(2,1)S(1)}, bf16[1,128,1024]{2,1,0:T(8,128)(2,1)S(1)}, u32[]{:S(2)}, u32[]{:S(2)}) collective-permute-start(bf16[1,128,1024]{2,1,0:T(8,128)(2,1)S(1)} %constant_dynamic-slice_fusion.5), channel_id=1, source_target_pairs={{0,16},{1,17},{2,18},{3,19},{4,20},{5,21},{6,22},{7,23},{8,24},{9,... | collective-permute-start | bytes 786440 | tf_op jit(solution)/shard_map/ppermute | solution.py:28
  279.4 7.3 %collective-permute-start.22 = (bf16[128,1024]{1,0:T(8,128)(2,1)S(1)}, bf16[128,1024]{1,0:T(8,128)(2,1)S(1)}, u32[]{:S(2)}, u32[]{:S(2)}) collective-permute-start(bf16[128,1024]{1,0:T(8,128)(2,1)S(1)} %get-tuple-element.29), channel_id=1, source_target_pairs={{0,0},{1,4},{2,1},{3,5},{4,2},{5,6},{6,3},{7,7},{8,8},{9,12},{10,9... | collective-permute-start | bytes 786440 | tf_op jit(solution)/shard_map/ppermute | solution.py:28
  280.1 15.0 %collective-permute-start.23 = (bf16[128,1024]{1,0:T(8,128)(2,1)S(1)}, bf16[128,1024]{1,0:T(8,128)(2,1)S(1)}, u32[]{:S(2)}, u32[]{:S(2)}) collective-permute-start(bf16[128,1024]{1,0:T(8,128)(2,1)S(1)} %get-tuple-element.28), channel_id=1, source_target_pairs={{0,4},{1,0},{2,5},{3,1},{4,6},{5,2},{6,7},{7,3},{8,12},{9,8},{10,1... | collective-permute-start | bytes 786440 | tf_op jit(solution)/shard_map/ppermute | solution.py:28
  295.6 17.7 %collective-permute-start.24 = (f32[128]{0:T(128)S(1)}, f32[128]{0:T(128)S(1)}, u32[]{:S(2)}, u32[]{:S(2)}) collective-permute-start(f32[128]{0:T(128)S(1)} %multiply_reduce_fusion), channel_id=1, source_target_pairs={{0,1},{1,2},{2,3},{3,0},{4,5},{5,6},{6,7},{7,4},{8,9},{9,10},{10,1... | collective-permute-start | bytes 1544 | tf_op jit(solution)/shard_map/ppermute | solution.py:28
  304.3 9.0 %collective-permute-start.25 = (f32[128]{0:T(128)S(1)}, f32[128]{0:T(128)S(1)}, u32[]{:S(2)}, u32[]{:S(2)}) collective-permute-start(f32[128]{0:T(128)S(1)} %multiply_reduce_fusion), channel_id=1, source_target_pairs={{0,2},{1,3},{2,0},{3,1},{4,6},{5,7},{6,4},{7,5},{8,10},{9,11},{10,... | collective-permute-start | bytes 1544 | tf_op jit(solution)/shard_map/ppermute | solution.py:28
  310.4 4.1 %collective-permute-start.26 = (f32[128]{0:T(128)S(1)}, f32[128]{0:T(128)S(1)}, u32[]{:S(2)}, u32[]{:S(2)}) collective-permute-start(f32[128]{0:T(128)S(1)} %multiply_reduce_fusion), channel_id=1, source_target_pairs={{0,3},{1,0},{2,1},{3,2},{4,7},{5,4},{6,5},{7,6},{8,11},{9,8},{10,9... | collective-permute-start | bytes 1544 | tf_op jit(solution)/shard_map/ppermute | solution.py:28
  (9 other events, 276.5 us)

commit v3 on v1

v3 whole, which is shorter than its diff:
```python
import math

import jax
import jax.numpy as jnp
from jax import lax
from jax.sharding import PartitionSpec as P

AXES = ("group", "dp", "tensor")

clip_rms = 0.5
beta_one = 0.9
beta_two = 0.95
bias_one = 1.0 - 0.9**10
bias_two = 1.0 - 0.95**10
adam_eps = 1e-08
learn_rate = 0.002


def permute(value, sizes, target):
    groups, ranks, slices = sizes
    index = lambda g, d, t: (g * ranks + d) * slices + t
    pairs = [
        (index(g, d, t), index(*target(g, d, t)))
        for g in range(groups)
        for d in range(ranks)
        for t in range(slices)
    ]
    return lax.ppermute(value, AXES, pairs)


def transpose_hidden(hidden, sizes):
    split = sizes[2] // sizes[0]
    return permute(hidden, sizes, lambda g, d, t: (t // split, d, g * split + t % split))


def gather_hidden(moved, sizes):
    groups, ranks, slices = sizes
    split = slices // groups
    rows, units = moved.shape
    full = lax.all_gather(moved, ("dp", "tensor"), axis=0, tiled=True)
    if split == 1:
        return full
    full = full.reshape(ranks * groups, split, rows, units).transpose(0, 2, 1, 3)
    return full.reshape(ranks * groups * rows, split * units)


def spread(part, sizes):
    groups, ranks, slices = sizes
    g, d, t = (lax.axis_index(axis) for axis in AXES)
    place = (d * slices + t) % ranks
    arrived = []
    for turn in range(ranks):

        def target(g, d, t, turn=turn):
            block = d * slices + t
            return (g, (block % ranks + turn) % ranks, block // ranks)

        sent = lax.dynamic_index_in_dim(part, (place + turn) % ranks, 0, keepdims=False)
        arrived.append(permute(sent, sizes, target))
    arrived = jnp.stack(arrived)
    ordered = [
        lax.dynamic_index_in_dim(arrived, (d - h) % ranks, 0, keepdims=False) for h in range(ranks)
    ]
    return jnp.concatenate(ordered, axis=1)


def per_device(weight, moment, second, gradient, hidden, stream, norm_gain):
    sizes = tuple(lax.axis_size(axis) for axis in AXES)
    groups, ranks, slices = sizes
    g, d, t = (lax.axis_index(axis) for axis in AXES)
    entries = weight.size * groups * ranks * slices
    width = stream.shape[1] * slices
    rows = stream.shape[0]

    lots = 2 if rows % 32 == 0 else 1
    height = rows // lots
    moved = [
        transpose_hidden(hidden[lot * height : (lot + 1) * height], sizes) for lot in range(lots)
    ]

    grad_float = gradient.astype(jnp.float32)
    squared = jnp.sum(grad_float * grad_float)
    squared, moved[-1] = lax.optimization_barrier((squared, moved[-1]))
    activations = [gather_hidden(lot, sizes) for lot in moved]
    grad_total = lax.psum(squared, AXES)
    factor = jnp.minimum(1.0, clip_rms * math.sqrt(entries) / (jnp.sqrt(grad_total) + 1e-06))
    clipped = factor * grad_float
    moment_new = beta_one * moment + (1.0 - beta_one) * clipped
    second_new = beta_two * second + (1.0 - beta_two) * clipped * clipped
    update = moment_new / bias_one / (jnp.sqrt(second_new / bias_two) + adam_eps)
    weight_new = weight - learn_rate * update
    shipped = weight_new.astype(jnp.bfloat16)

    cols = shipped.shape[1]
    summed = []
    part = None
    for lot in activations:
        if part is not None:
            part, lot = lax.optimization_barrier((part, lot))
            summed.append(spread(part, sizes))
        term = jnp.dot(lot, shipped, preferred_element_type=jnp.float32)
        part = term.astype(jnp.bfloat16)

        step = 1
        while step < groups:
            bit = (g // step) % 2
            pairs = part.reshape(-1, 2, height, cols)
            kept = lax.dynamic_index_in_dim(pairs, bit, 1, keepdims=False)
            sent = lax.dynamic_index_in_dim(pairs, 1 - bit, 1, keepdims=False)
            got = permute(sent, sizes, lambda g, d, t, step=step: (g ^ step, d, t))
            part = (kept.astype(jnp.float32) + got.astype(jnp.float32)).astype(jnp.bfloat16)
            step *= 2
        part = part.reshape(ranks, height, cols)
    summed.append(spread(part, sizes))
    summed = jnp.concatenate(summed, axis=0)

    residual_sum = stream.astype(jnp.float32) + summed.astype(jnp.float32)
    squares = lax.psum(jnp.sum(residual_sum * residual_sum, axis=1), "tensor")
    normed = residual_sum * lax.rsqrt(squares / width + 1e-06)[:, None] * norm_gain.astype(jnp.float32)
    return (
        weight_new,
        moment_new,
        second_new,
        normed.astype(jnp.bfloat16),
        residual_sum.astype(jnp.bfloat16),
    )


def solution(mesh):
    master = P("group", ("dp", "tensor"))
    decode = P(("group", "dp"), "tensor")
    return jax.shard_map(
        per_device,
        mesh=mesh,
        in_specs=(master, master, master, master, decode, decode, P("tensor")),
        out_specs=(master, master, master, decode, decode),
        check_vma=False,
    )
```

time: 269 us -> 248 us (0.922)
  waiting for transfers between devices: 66.8 us -> 29.1 us
  blocking collectives: 107 us -> 119 us
  matrix products: 13.8 us -> 21.4 us
  local copies, waits for them, and re-layouts: 9.65 us -> 2.2 us
  starting transfers between devices: 8.6 us -> 15.7 us
  other arithmetic: 47.6 us -> 44.2 us
    ppermute x5 -> x10, waiting for transfers between devices: 35.7 us -> 16.1 us  [permute(): return lax.ppermute(value, AXES, pairs)]
    all_gather x1 -> x2, waiting for transfers between devices: 31.1 us -> 13 us  [gather_hidden(): full = lax.all_gather(moved, ('dp', 'tensor'), axis=0, tiled=True)]
    psum x1, blocking collectives: 88.7 us -> 101 us  [per_device(): grad_total = lax.psum(squared, AXES)]
    dot_general x1 -> x2, matrix products: 13.8 us -> 21.4 us  [per_device(): term = jnp.dot(lot, shipped, preferred_element_type=jnp.float32)]
    ppermute x5 -> x10, starting transfers between devices: 8.57 us -> 15.6 us  [permute(): return lax.ppermute(value, AXES, pairs)]
    dynamic_update_slice x2 -> x0, local copies, waits for them, and re-layouts: 7.07 us -> none  [per_device(): summed = lax.dynamic_update_index_in_dim(summed, got, (d - turn) % ranks, 0)]
  transfers between devices with their start and end apart: 6 -> 12, of which waited for: 4 -> 6; matrix products, arithmetic and copies ran while one was open for 16% -> 22% of each run, Pallas kernels for 0% -> 0%
where the time goes in v3:
time: 248 us; the launch traced here: 247 us
  blocking collectives  119 us (48%)
  other arithmetic  44.2 us (18%)
  waiting for transfers between devices  29.1 us (12%)
  matrix products  21.4 us (9%)
  starting transfers between devices  15.7 us (6%)
  between operations  15.1 us (6%)
    psum x1, blocking collectives, per_device(): grad_total = lax.psum(squared, AXES)  101 us
    sub x1, other arithmetic, per_device(): weight_new = weight - learn_rate * update  34.3 us
    dot_general x2, matrix products, per_device(): term = jnp.dot(lot, shipped, preferred_element_type=jnp.float32)  21.4 us
    psum x1, blocking collectives, per_device(): squares = lax.psum(jnp.sum(residual_sum * residual_sum, axis=1), 'tensor')  18.1 us
    ppermute x10, waiting for transfers between devices, permute(): return lax.ppermute(value, AXES, pairs)  16.1 us
    ppermute x10, starting transfers between devices, permute(): return lax.ppermute(value, AXES, pairs)  15.6 us
    all_gather x2, waiting for transfers between devices, gather_hidden(): full = lax.all_gather(moved, ('dp', 'tensor'), axis=0, tiled=True)  13 us
    reduce_sum x1, other arithmetic, per_device(): squared = jnp.sum(grad_float * grad_float)  7.67 us
  transfers between devices with their start and end apart: 12, of which 6 were waited for; matrix products, arithmetic and copies ran while one was open for 22% of the time, Pallas kernels for 0%

profile of v3, /device:TPU:0, one launch (start us, length us, event | category | flops | bytes accessed | tf_op | source)
XLA Modules:
  0.0 247.2 jit_solution(6525044272368266674)
XLA Ops:
  7.2 1.2 fusion.29
  8.4 0.7 collective-permute-start.1
  9.2 0.8 copy-done.2
  10.0 0.7 collective-permute-start
  10.7 7.7 %fusion.2 = f32[]{:T(128)} fusion(bf16[3712,1024]{1,0:T(8,128)(2,1)} %param.10), kind=kLoop, calls=%fused_computation.5 | loop fusion | flops 11403263 | bytes 7602180 | tf_op jit(solution)/shard_map/reduce_sum | solution.py:82
  18.4 101.3 %psum.14 = f32[]{:T(128)} all-reduce(f32[]{:T(128)} %fusion.2), channel_id=1, replica_groups=mesh['group'=4,'dp'=2,'tensor'=4] {'group','dp','tensor'}, use_global_device_ids=true, to_apply=%region_1.0 | all-reduce | flops 1 | bytes 8 | tf_op jit(solution)/shard_map/psum | solution.py:85
  120.5 34.3 %multiply_subtract_fusion = (f32[3712,1024]{1,0:T(8,128)}, f32[3712,1024]{1,0:T(8,128)}, f32[3712,1024]{1,0:T(8,128)}) fusion(f32[3712,1024]{1,0:T(8,128)} %param.7, bf16[3712,1024]{1,0:T(8,128)(2,1)} %param.10, f32[]{:T(128)S(6)} %min_shard_map.3, f32[3712,1024]{1,0:T(8,128)} %param.8, f32[3712,1024]{1,0:T(8,128)} %param.9), kind=kLoop, calls=%fused_computation.7 | loop fusion | flops 57016320 | bytes 98828288 | tf_op jit(solution)/shard_map/sub | solution.py:91
  154.8 10.7 %fusion.8 = bf16[1024,512]{0,1:T(8,128)(2,1)S(1)} fusion(bf16[512,3712]{1,0:T(8,128)(2,1)} %all-gather.3.cloned.1.call-done, f32[3712,1024]{1,0:T(8,128)} %get-tuple-element.13), kind=kOutput, calls=%fused_computation.12 | convolution fusion | flops 3896639488 | bytes 20054016 | tf_op jit(solution)/shard_map/dot_general | solution.py:101
  165.7 1.9 collective-permute-done.2
  167.8 2.3 collective-permute-start.3
  170.1 6.6 %collective-permute-done.3 = bf16[2,64,1024]{2,1,0:T(8,128)(2,1)S(1)} collective-permute-done((bf16[2,64,1024]{2,1,0:T(8,128)(2,1)S(1)}, bf16[2,64,1024]{2,1,0:T(8,128)(2,1)S(1)}, u32[]{:S(2)}, u32[]{:S(2)}) %collective-permute-start.3) | collective-permute-done | bytes 262176 | tf_op jit(solution)/shard_map/ppermute | solution.py:28
  176.8 13.0 %all-gather.5.cloned.1.call-done = bf16[512,3712]{1,0:T(8,128)(2,1)} async-done(((bf16[64,3712]{1,0:T(8,128)(2,1)}), bf16[512,3712]{1,0:T(8,128)(2,1)}) %all-gather.5.cloned.1.call-update) | async-done | bytes 3801104 | tf_op jit(solution)/shard_map/all_gather | solution.py:40
  189.7 10.7 %fusion.11 = bf16[512,1024]{1,0:T(8,128)(2,1)S(1)} fusion(bf16[512,3712]{1,0:T(8,128)(2,1)} %all-gather.5.cloned.1.call-done, f32[3712,1024]{1,0:T(8,128)} %get-tuple-element.13), kind=kOutput, calls=%fused_computation.13 | convolution fusion | flops 3896639488 | bytes 20054016 | tf_op jit(solution)/shard_map/dot_general | solution.py:101
  200.6 1.9 collective-permute-done.6
  202.7 1.5 collective-permute-start.7
  204.3 0.7 collective-permute-start.4
  204.9 4.5 %collective-permute-start.5 = (bf16[64,1024]{1,0:T(8,128)(2,1)S(1)}, bf16[64,1024]{1,0:T(8,128)(2,1)S(1)}, u32[]{:S(2)}, u32[]{:S(2)}) collective-permute-start(bf16[64,1024]{1,0:T(8,128)(2,1)S(1)} %get-tuple-element.22), channel_id=1, source_target_pairs={{0,4},{1,0},{2,5},{3,1},{4,6},{5,2},{6,7},{7,3},{8,12},{9,8},{10,1... | collective-permute-start | bytes 393224 | tf_op jit(solution)/shard_map/ppermute | solution.py:28
  209.4 1.7 collective-permute-done.7
  211.2 0.7 collective-permute-start.8
  211.9 4.5 %collective-permute-start.9 = (bf16[64,1024]{1,0:T(8,128)(2,1)S(1)}, bf16[64,1024]{1,0:T(8,128)(2,1)S(1)}, u32[]{:S(2)}, u32[]{:S(2)}) collective-permute-start(bf16[64,1024]{1,0:T(8,128)(2,1)S(1)} %get-tuple-element.26), channel_id=1, source_target_pairs={{0,4},{1,0},{2,5},{3,1},{4,6},{5,2},{6,7},{7,3},{8,12},{9,8},{10,1... | collective-permute-start | bytes 393224 | tf_op jit(solution)/shard_map/ppermute | solution.py:28
  216.5 4.1 %collective-permute-done.9 = bf16[64,1024]{1,0:T(8,128)(2,1)S(1)} collective-permute-done((bf16[64,1024]{1,0:T(8,128)(2,1)S(1)}, bf16[64,1024]{1,0:T(8,128)(2,1)S(1)}, u32[]{:S(2)}, u32[]{:S(2)}) %collective-permute-start.9) | collective-permute-done | bytes 131104 | tf_op jit(solution)/shard_map/ppermute | solution.py:28
  220.7 0.3 multiply_reduce_fusion
  221.0 18.1 %psum.15 = f32[128]{0:T(128)S(1)} all-reduce(f32[128]{0:T(128)S(1)} %multiply_reduce_fusion), channel_id=1, replica_groups=mesh['group'=4,'dp'=2,'tensor'=4] {'tensor'}, use_global_device_ids=true, to_apply=%region_3.4 | all-reduce | flops 128 | bytes 1024 | tf_op jit(solution)/shard_map/psum | solution.py:118
  239.2 1.2 fusion.16
  (33 shorter events, 1.2 us)
Async XLA Ops:
  7.2 147.6 %all-gather.3.cloned.1.call-start = ((), (), s32[]{:S(2)}) async-start(), calls=%async_computation | async-start | bytes 4276224 | tf_op jit(solution)/shard_map/all_gather | solution.py:40
  8.4 0.7 collective-permute-start.1
  9.2 0.8 copy-start.2
  10.0 179.8 %all-gather.5.cloned.1.call-start = ((), (), s32[]{:S(2)}) async-start(), calls=%async_computation.1 | async-start | bytes 4276224 | tf_op jit(solution)/shard_map/all_gather | solution.py:40
  10.0 8.4 %collective-permute-start = (bf16[64,3712]{1,0:T(8,128)(2,1)S(1)}, bf16[64,3712]{1,0:T(8,128)(2,1)S(1)}, u32[]{:S(2)}, u32[]{:S(2)}) collective-permute-start(bf16[64,3712]{1,0:T(8,128)(2,1)S(1)} %get-tuple-element.19), channel_id=1, source_target_pairs={{0,0},{1,8},{2,16},{3,24},{4,4},{5,12},{6,20},{7,28},{8,1},{9,9},{... | collective-permute-start | bytes 1425416 | tf_op jit(solution)/shard_map/ppermute | solution.py:28
  18.4 102.0 %copy-start.1 = (bf16[64,3712]{1,0:T(8,128)(2,1)}, bf16[64,3712]{1,0:T(8,128)(2,1)S(1)}, u32[]{:S(2)}) copy-start(bf16[64,3712]{1,0:T(8,128)(2,1)S(1)} %collective-permute-done) | copy-start | bytes 1425412
  165.6 2.0 collective-permute-start.2
  167.8 8.9 %collective-permute-start.3 = (bf16[2,64,1024]{2,1,0:T(8,128)(2,1)S(1)}, bf16[2,64,1024]{2,1,0:T(8,128)(2,1)S(1)}, u32[]{:S(2)}, u32[]{:S(2)}) collective-permute-start(bf16[2,64,1024]{2,1,0:T(8,128)(2,1)S(1)} %dynamic-slice_bitcast_fusion.3), channel_id=1, source_target_pairs={{0,16},{1,17},{2,18},{3,19},{4,20},{5,21},{6,22},{7,23},{8,24},{9,... | collective-permute-start | bytes 786440 | tf_op jit(solution)/shard_map/ppermute | solution.py:28
  176.8 39.6 %copy-start.3 = (bf16[2048]{0:T(1024)(128)(2,1)S(1)}, bf16[2048]{0:T(1024)(128)(2,1)}, u32[]{:S(2)}) copy-start(bf16[2048]{0:T(1024)(128)(2,1)} %param.13) | copy-start | bytes 12292
  176.8 44.0 %copy-start = (bf16[128,2048]{1,0:T(8,128)(2,1)S(1)}, bf16[128,2048]{1,0:T(8,128)(2,1)}, u32[]{:S(2)}) copy-start(bf16[128,2048]{1,0:T(8,128)(2,1)} %param.12) | copy-start | bytes 1572868
  200.5 2.0 collective-permute-start.6
  202.7 8.4 %collective-permute-start.7 = (bf16[2,64,1024]{2,1,0:T(8,128)(2,1)S(1)}, bf16[2,64,1024]{2,1,0:T(8,128)(2,1)S(1)}, u32[]{:S(2)}, u32[]{:S(2)}) collective-permute-start(bf16[2,64,1024]{2,1,0:T(8,128)(2,1)S(1)} %dynamic-slice_bitcast_fusion.2), channel_id=1, source_target_pairs={{0,16},{1,17},{2,18},{3,19},{4,20},{5,21},{6,22},{7,23},{8,24},{9,... | collective-permute-start | bytes 786440 | tf_op jit(solution)/shard_map/ppermute | solution.py:28
  204.3 12.1 %collective-permute-start.4 = (bf16[64,1024]{1,0:T(8,128)(2,1)S(1)}, bf16[64,1024]{1,0:T(8,128)(2,1)S(1)}, u32[]{:S(2)}, u32[]{:S(2)}) collective-permute-start(bf16[64,1024]{1,0:T(8,128)(2,1)S(1)} %get-tuple-element.23), channel_id=1, source_target_pairs={{0,0},{1,4},{2,1},{3,5},{4,2},{5,6},{6,3},{7,7},{8,8},{9,12},{10,9... | collective-permute-start | bytes 393224 | tf_op jit(solution)/shard_map/ppermute | solution.py:28
  204.9 11.5 %collective-permute-start.5 = (bf16[64,1024]{1,0:T(8,128)(2,1)S(1)}, bf16[64,1024]{1,0:T(8,128)(2,1)S(1)}, u32[]{:S(2)}, u32[]{:S(2)}) collective-permute-start(bf16[64,1024]{1,0:T(8,128)(2,1)S(1)} %get-tuple-element.22), channel_id=1, source_target_pairs={{0,4},{1,0},{2,5},{3,1},{4,6},{5,2},{6,7},{7,3},{8,12},{9,8},{10,1... | collective-permute-start | bytes 393224 | tf_op jit(solution)/shard_map/ppermute | solution.py:28
  211.2 5.3 %collective-permute-start.8 = (bf16[64,1024]{1,0:T(8,128)(2,1)S(1)}, bf16[64,1024]{1,0:T(8,128)(2,1)S(1)}, u32[]{:S(2)}, u32[]{:S(2)}) collective-permute-start(bf16[64,1024]{1,0:T(8,128)(2,1)S(1)} %get-tuple-element.27), channel_id=1, source_target_pairs={{0,0},{1,4},{2,1},{3,5},{4,2},{5,6},{6,3},{7,7},{8,8},{9,12},{10,9... | collective-permute-start | bytes 393224 | tf_op jit(solution)/shard_map/ppermute | solution.py:28
  211.9 8.7 %collective-permute-start.9 = (bf16[64,1024]{1,0:T(8,128)(2,1)S(1)}, bf16[64,1024]{1,0:T(8,128)(2,1)S(1)}, u32[]{:S(2)}, u32[]{:S(2)}) collective-permute-start(bf16[64,1024]{1,0:T(8,128)(2,1)S(1)} %get-tuple-element.26), channel_id=1, source_target_pairs={{0,4},{1,0},{2,5},{3,1},{4,6},{5,2},{6,7},{7,3},{8,12},{9,8},{10,1... | collective-permute-start | bytes 393224 | tf_op jit(solution)/shard_map/ppermute | solution.py:28
Sparse Core Ops, SparseCore 0:
  10.7 108.5 all-gather.2
  122.0 67.6 all-gather.4
